TPU v7x, 128 devices: a whole 4x4x4 slice. The times are simulated.
128 devices in a mesh: rep: 32 (over x, z, core), tp: 4 (over y).
Axes of the slice: x: 4, y: 4, z: 4, core: 2. Of those that a mesh axis runs over, the one named last changes fastest.
Arguments:
- hidden_in: bfloat16 [49152, 5120], P('rep', 'tp'), may hold values from -6 to 6
- ln_gain: float32 [5120], replicated, may hold values from 0.5 to 1.5
- w_query: bfloat16 [5120, 4096], P(None, 'tp'), may hold values from -0.078125 to 0.078125
- key_value_weight: bfloat16 [5120, 4, 256], P(None, 'tp'), may hold values from -0.078125 to 0.078125
- q_gain: float32 [128], replicated, may hold values from 0.25 to 1.75
- k_gain: float32 [128], replicated, may hold values from 0.25 to 1.75
- key_value_cache: bfloat16 [2048, 64, 4, 256], P('rep', None, 'tp'), may hold values from -256 to 256
- prefix_pages: int32 [32, 4], replicated, may hold values from 1 to 16, as said below
- page_holder: int32 [32, 4, 16], replicated, may hold values from 0 to 31, as said below
- page_slot: int32 [32, 4, 16], replicated, may hold values from 0 to 63
- span_pages: int32 [32, 4], replicated, may hold values from 1 to 12, 24 in all within a row
- decode_target: int32 [32, 24, 1], replicated, may hold values from 0 to 31; in each aligned block of 24 rows (0 to 23, 24 to 47, ..., all dimensions but the last counted through in order) at most 2 rows name the same one
Outputs:
- attn_out: bfloat16 [49152, 4096], P('rep', 'tp')
- pushed: bfloat16 [2048, 64, 4, 256], P('rep', None, 'tp')
Inputs may be any that keep to these rules, and one draw needn't show every extreme that they name: `prefix_pages`: in every draw some replica has all its sessions at 16 pages. `page_holder`: of the 64 page positions of one replica's sessions, used or not, exactly 2 name each holder. `span_pages`: each replica's row sums to 24 and its largest entry is 12. `decode_target`: among the 24 pages of one replica no decode replica is named more than 2 times, and in some replica one is named exactly 2 times.
All inputs are finite; a program needn't handle non-finite values.
Results may differ from a plain program's by a relative error of at most 0.0045.
The roundings to bfloat16 on the way count: a program that leaves them out, or rounds other values in their place, can miss the bound.
Values may be sent and summed in bfloat16 or wider, within the bound.
No kernel may reach another device: no remote copies, remote signals or barrier semaphores. Data moves between devices by JAX's collectives and lax.ppermute only.
A program may use at most 192 MiB of HBM per device.

v0:
```python
import jax
import jax.numpy as jnp
from jax import lax
from jax.sharding import PartitionSpec as P


def rms_scale(values, gain):
    mean_square = jnp.mean(values * values, axis=-1, keepdims=True)
    return values * lax.rsqrt(mean_square + 1e-06) * gain


def rotary(values, positions):
    half_dim = values.shape[-1] // 2
    exponent = jnp.arange(half_dim, dtype=jnp.float32) * (2.0 / values.shape[-1])
    inverse = jnp.power(jnp.float32(1000000.0), -exponent)
    angles = positions.astype(jnp.float32)[:, None] * inverse[None, :]
    cosine = jnp.concatenate([jnp.cos(angles), jnp.cos(angles)], -1)[:, None, :]
    sine = jnp.concatenate([jnp.sin(angles), jnp.sin(angles)], -1)[:, None, :]
    rotated = jnp.concatenate([-values[..., half_dim:], values[..., :half_dim]], -1)
    return values * cosine + rotated * sine


def page_layout(span_counts, prefix_counts, page_count):
    ends = jnp.cumsum(span_counts, axis=1)
    starts = ends - span_counts
    page_index = jnp.arange(page_count, dtype=jnp.int32)
    session_of = jnp.sum((page_index[None, :, None] >= ends[:, None, :]).astype(jnp.int32), -1)
    onehot = session_of[..., None] == jnp.arange(span_counts.shape[1], dtype=jnp.int32)
    start_of = jnp.sum(jnp.where(onehot, starts[:, None, :], 0), -1)
    prefix_of = jnp.sum(jnp.where(onehot, prefix_counts[:, None, :], 0), -1)
    return (session_of, start_of, prefix_of, starts)


def target_ranks(targets):
    count = targets.shape[1]
    order = jnp.arange(count, dtype=jnp.int32)
    earlier = (targets[:, :, None] == targets[:, None, :]) & (
        order[None, None, :] < order[None, :, None]
    )
    return jnp.sum(earlier.astype(jnp.int32), -1)


def key_mask(page_number, start_page, prefix_count, max_pages, most_pages, page_size):
    key_page = jnp.arange(max_pages + most_pages, dtype=jnp.int32)
    relative = page_number - start_page
    within = key_page - max_pages
    query_row = jnp.arange(page_size, dtype=jnp.int32)
    causal = query_row[None, :] <= query_row[:, None]
    prefix_ok = (key_page < prefix_count)[None, :, None]
    span_page = (key_page >= max_pages)[None, :, None]
    earlier = (within < relative)[None, :, None]
    diagonal = (within == relative)[None, :, None] & causal[:, None, :]
    visible = prefix_ok | span_page & (earlier | diagonal)
    return visible.reshape(page_size, -1)


def attend(query_page, key_rows, visible):
    page_size, head_count, head_dim = query_page.shape
    group_heads = key_rows.shape[1]
    grouped = query_page.reshape(page_size, group_heads, -1, head_dim)
    scores = jnp.einsum(
        "qhgd,khd->hgqk", grouped, key_rows[..., :head_dim], preferred_element_type=jnp.float32
    )
    scores = scores / jnp.sqrt(jnp.float32(head_dim))
    scores = jnp.where(visible[None, None], scores, -jnp.inf)
    top = jnp.max(scores, axis=-1, keepdims=True)
    weights = jnp.exp(scores - top)
    probs = (weights / jnp.sum(weights, axis=-1, keepdims=True)).astype(jnp.bfloat16)
    mixed = jnp.einsum(
        "hgqk,khd->qhgd", probs, key_rows[..., head_dim:], preferred_element_type=jnp.float32
    )
    return mixed.astype(jnp.bfloat16).reshape(page_size, -1)


def per_device(
    hidden_in,
    ln_gain,
    w_query,
    key_value_weight,
    q_gain,
    k_gain,
    key_value_cache,
    prefix_pages,
    page_holder,
    page_slot,
    span_pages,
    decode_target,
):
    replica = lax.axis_index("rep")
    replicas = lax.axis_size("rep")
    gathered = lax.all_gather(hidden_in, "tp", axis=1, tiled=True)
    head_dim = q_gain.shape[0]
    page_size = key_value_cache.shape[1]
    local_heads = key_value_cache.shape[2]
    row_count = gathered.shape[0]
    page_count = row_count // page_size
    sessions = span_pages.shape[1]
    max_pages = page_holder.shape[2]
    most_pages = page_count // 2
    capacity = sessions * max_pages // replicas
    push_slots = max(2, (page_count + replicas - 1) // replicas)
    entry_shape = (page_size, local_heads, 2 * head_dim)
    normalized_input = rms_scale(gathered.astype(jnp.float32), ln_gain).astype(jnp.bfloat16)
    query = jnp.dot(normalized_input, w_query, preferred_element_type=jnp.float32).reshape(
        row_count, -1, head_dim
    )
    key_value_rows = jnp.dot(
        normalized_input,
        key_value_weight.reshape(key_value_weight.shape[0], -1),
        preferred_element_type=jnp.float32,
    )
    key_value_rows = key_value_rows.reshape(row_count, local_heads, 2 * head_dim)
    session_all, start_all, prefix_all, starts = page_layout(span_pages, prefix_pages, page_count)
    my_session = lax.dynamic_index_in_dim(session_all, replica, 0, keepdims=False)
    my_start = lax.dynamic_index_in_dim(start_all, replica, 0, keepdims=False)
    my_prefix = lax.dynamic_index_in_dim(prefix_all, replica, 0, keepdims=False)
    page_index = jnp.arange(page_count, dtype=jnp.int32)
    page_base = (my_prefix + page_index - my_start) * page_size
    positions = (page_base[:, None] + jnp.arange(page_size, dtype=jnp.int32)[None, :]).reshape(-1)
    query_rot = rotary(rms_scale(query, q_gain), positions).astype(jnp.bfloat16)
    rotated_key = rotary(rms_scale(key_value_rows[..., :head_dim], k_gain), positions).astype(
        jnp.bfloat16
    )
    fresh_value_rows = key_value_rows[..., head_dim:].astype(jnp.bfloat16)
    fresh = jnp.concatenate([rotated_key, fresh_value_rows], -1).reshape(
        (page_count,) + entry_shape
    )
    position_count = sessions * max_pages
    flat_holder = page_holder.reshape(replicas, position_count)
    flat_slot = page_slot.reshape(replicas, position_count)
    page_pos = jnp.arange(max_pages, dtype=jnp.int32)
    used = (page_pos[None, None, :] < prefix_pages[:, :, None]).reshape(replicas, position_count)
    from_here = used & (flat_holder == replica)
    send_rank = jnp.cumsum(from_here.astype(jnp.int32), axis=1) - 1
    slot_range = jnp.arange(capacity, dtype=jnp.int32)
    matched = from_here[:, None, :] & (send_rank[:, None, :] == slot_range[None, :, None])
    local_ids = jnp.sum(jnp.where(matched, flat_slot[:, None, :], 0), -1)
    present = jnp.any(matched, axis=-1)
    outgoing = jnp.take(key_value_cache, local_ids.reshape(-1), axis=0).reshape(
        (replicas, capacity) + entry_shape
    )
    outgoing = jnp.where(present[:, :, None, None, None], outgoing, jnp.zeros_like(outgoing))
    incoming = lax.all_to_all(outgoing, "rep", split_axis=0, concat_axis=0, tiled=True)
    incoming = incoming.reshape((replicas * capacity,) + entry_shape)
    my_holder = lax.dynamic_index_in_dim(flat_holder, replica, 0, keepdims=False)
    my_used = lax.dynamic_index_in_dim(used, replica, 0, keepdims=False)
    position_index = jnp.arange(position_count, dtype=jnp.int32)
    same_earlier = (
        (my_holder[:, None] == my_holder[None, :])
        & my_used[None, :]
        & (position_index[None, :] < position_index[:, None])
    )
    recv_rank = jnp.sum(same_earlier.astype(jnp.int32), axis=1)
    recv_ids = jnp.where(my_used, my_holder * capacity + recv_rank, 0)
    fetched_pages = jnp.take(incoming, recv_ids, axis=0)
    fetched_pages = jnp.where(
        my_used[:, None, None, None], fetched_pages, jnp.zeros_like(fetched_pages)
    )
    fetched_pages = fetched_pages.reshape((sessions, max_pages) + entry_shape)
    query_pages = query_rot.reshape(page_count, page_size, -1, head_dim)

    def one_page(page_items):
        page_number, query_page, session, start_page, prefix_count = page_items
        prefix_key_rows = lax.dynamic_index_in_dim(fetched_pages, session, 0, keepdims=False)
        span_ids = jnp.clip(start_page + jnp.arange(most_pages, dtype=jnp.int32), 0, page_count - 1)
        span_key_rows = jnp.take(fresh, span_ids, axis=0)
        key_rows = jnp.concatenate([prefix_key_rows, span_key_rows], 0).reshape(
            -1, local_heads, 2 * head_dim
        )
        visible = key_mask(page_number, start_page, prefix_count, max_pages, most_pages, page_size)
        return attend(query_page, key_rows, visible)

    attn_out = lax.map(one_page, (page_index, query_pages, my_session, my_start, my_prefix))
    attn_out = attn_out.reshape(row_count, -1)
    targets = decode_target[..., 0]
    ranks = target_ranks(targets)
    slot_order = jnp.arange(push_slots, dtype=jnp.int32)
    everyone = lax.all_gather(fresh, "rep", axis=0, tiled=True)
    source_range = jnp.arange(replicas, dtype=jnp.int32)
    chosen = (targets[:, None, :] == replica) & (ranks[:, None, :] == slot_order[None, :, None])
    take_ids = source_range[:, None] * page_count + jnp.sum(
        jnp.where(chosen, page_index[None, None, :], 0), -1
    )
    take_valid = jnp.any(chosen, axis=-1).reshape(-1)
    pushed = jnp.take(everyone, take_ids.reshape(-1), axis=0)
    pushed = jnp.where(take_valid[:, None, None, None], pushed, jnp.zeros_like(pushed))
    return (attn_out, pushed)


def solution(mesh):
    placed = (
        P("rep", "tp"),
        P(),
        P(None, "tp"),
        P(None, "tp", None),
        P(),
        P(),
        P("rep", None, "tp", None),
        P(),
        P(),
        P(),
        P(),
        P(),
    )
    return jax.shard_map(
        per_device,
        mesh=mesh,
        in_specs=placed,
        out_specs=(P("rep", "tp"), P("rep", None, "tp", None)),
        check_vma=False,
    )
```

profile of v0, /device:TPU:125, one launch (start us, length us, event | category | flops | bytes accessed | tf_op | source)
XLA Modules:
  0.0 611.2 jit_solution(16577868538894334753)
XLA Ops:
  9.2 3.6 gather_fusion.2
  12.8 1.8 bitcast_select_fusion.4
  14.7 1.5 broadcast_select_fusion
  16.2 7.5 %all-to-all-start = ((bf16[32,2,64,1,256]{4,2,1,3,0:T(8,128)(2,1)}), bf16[32,2,64,1,256]{4,2,1,3,0:T(8,128)(2,1)}, u32[]{:S(2)}, u32[]{:S(2)}) async-start(bf16[32,2,64,1,256]{4,2,1,3,0:T(8,128)(2,1)} %broadcast_select_fusion), calls=%async_computation | async-start | bytes 4194304 | tf_op jit(solution)/shard_map/all_to_all | solution.py:143
  25.8 2.8 multiply_cosine_fusion
  30.9 1.4 fusion.33
  32.4 15.9 %all-to-all-done = bf16[32,2,64,1,256]{4,2,1,3,0:T(8,128)(2,1)} async-done(((bf16[32,2,64,1,256]{4,2,1,3,0:T(8,128)(2,1)}), bf16[32,2,64,1,256]{4,2,1,3,0:T(8,128)(2,1)}, u32[]{:S(2)}, u32[]{:S(2)}) %all-to-all-start) | async-done | bytes 2097184 | tf_op jit(solution)/shard_map/all_to_all | solution.py:143
  48.2 3.6 gather_fusion.3
  51.8 3.3 fusion.29
  55.1 99.8 %all-gather.3.cloned.1.call-done = bf16[1536,5120]{1,0:T(8,128)(2,1)} async-done(((bf16[1536,1280]{1,0:T(8,128)(2,1)}), bf16[1536,5120]{1,0:T(8,128)(2,1)}) %all-gather.3.cloned.1.call-update) | async-done | bytes 15728656 | tf_op jit(solution)/shard_map/all_gather | solution.py:91
  154.9 6.9 %fusion.12 = f32[1536]{0:T(1024)S(1)} fusion(bf16[1536,5120]{1,0:T(8,128)(2,1)} %all-gather.3.cloned.1.call-done), kind=kLoop, calls=%fused_computation.34 | loop fusion | flops 23591424 | bytes 15734784 | tf_op jit(solution)/shard_map/reduce_sum | solution.py:8
  161.9 8.7 %fusion.23 = f32[1536,1,256]{0,2,1:T(8,128)S(1)} fusion(bf16[1536,5120]{1,0:T(8,128)(2,1)} %all-gather.3.cloned.1.call-done, f32[5120]{0:T(1024)S(1)} %copy-done.12, f32[1536]{0:T(1024)S(1)} %add_rsqrt_fusion.2, bf16[5120,1,256]{2,0,1:T(8,128)(2,1)S(1)} %copy-done), kind=kOutput, calls=%fused_computation.48 | convolution fusion | flops 4057989120 | bytes 19949568 | tf_op jit(solution)/shard_map/dot_general | solution.py:107
  172.4 24.5 %multiply_reduce_fusion = (f32[1536,8]{0,1:T(8,128)S(1)}, f32[1536,1024]{0,1:T(8,128)}) fusion(bf16[5120,1024]{1,0:T(8,128)(2,1)} %param.18, bf16[1536,5120]{1,0:T(8,128)(2,1)} %all-gather.3.cloned.1.call-done, f32[5120]{0:T(1024)S(1)} %copy-done.12, f32[1536]{0:T(1024)S(1)} %add_rsqrt_fusion.2), kind=kOutput, calls=%fused_computation.44 | convolution fusion | flops 16140718080 | bytes 32581632 | tf_op jit(solution)/shard_map/dot_general | solution.py:104
  196.9 6.6 %copy.107 = f32[1536,1024]{1,0:T(8,128)} copy(f32[1536,1024]{0,1:T(8,128)} %get-tuple-element.219) | data formatting | bytes 12582912 | tf_op jit(solution)/shard_map/dot_general | solution.py:104
  203.8 3.8 multiply_multiply_fusion
  207.6 3.4 slice_negate_fusion
  211.0 5.8 copy.119
  216.9 5.8 copy.120
  222.7 7.1 %copy.122 = f32[192,8,8,128]{3,2,1,0:T(8,128)} copy(f32[192,8,8,128]{3,1,2,0:T(8,128)} %bitcast.148) | data formatting | bytes 12582912
  229.9 9.9 %fusion.18 = bf16[24,64,8,128]{3,2,1,0:T(8,128)(2,1)} fusion(f32[24,64,8,64]{3,2,1,0:T(8,128)} %bitcast.150, f32[24,64,8,64]{3,2,1,0:T(8,128)} %bitcast.149, f32[24,64,128]{2,1,0:T(8,128)S(1)} %copy-done.4, f32[24,64,128]{2,1,0:T(8,128)S(1)} %copy-done.3, f32[128]{0:T(128)S(1)} %copy-done.11, f32[24,64,8]{2,1,0:T(8,128)S(1)} %bitcast.158, ...), kind=kLoop, calls=%fused_computation.41 | loop fusion | flops 11010048 | bytes 17351168 | tf_op jit(solution)/shard_map/convert_element_type | solution.py:120
  239.8 351.0 %while.12 = (s32[]{:T(128)}, bf16[24,64,1024]{2,1,0:T(8,128)(2,1)}, s32[24]{0:T(128)S(1)}, bf16[4,16,64,1,256]{4,2,1,3,0:T(8,128)(2,1)}, s32[24]{0:T(128)S(1)}, ...) while((s32[]{:T(128)}, bf16[24,64,1024]{2,1,0:T(8,128)(2,1)}, ...), condition=%wide.region_14.16_spmd, body=%wide.region_11.15_spmd.sunk | while | flops 478286144 | bytes 18439284 | solution.py:173
  286.2 1.2 dynamic-slice_bitcast_fusion.2
  590.8 10.3 %gather_fusion.1 = bf16[64,64,256]{2,1,0:T(8,128)(2,1)} fusion(bf16[768,64,256]{2,1,0:T(8,128)(2,1)} %bitcast.160, s32[1024]{0:T(1024)S(1)} %pad_clamp_fusion.1), kind=kCustom, calls=%fused_computation.3 | custom fusion | bytes 4194560 | tf_op jit(solution)/shard_map/jit(_take)/gather | solution.py:185
  601.1 3.2 fusion.28
  (883 shorter events, 281.5 us)
Async XLA Ops:
  7.2 154.7 %copy-start = (bf16[5120,1,256]{2,0,1:T(8,128)(2,1)S(1)}, bf16[5120,1,256]{2,0,1:T(8,128)(2,1)}, u32[]{:S(2)}) copy-start(bf16[5120,1,256]{2,0,1:T(8,128)(2,1)} %param.19) | copy-start | bytes 7864324
  7.2 0.9 copy-start.8
  7.2 0.9 copy-start.5
  7.2 1.1 copy-start.7
  7.2 147.7 %all-gather.3.cloned.1.call-start = ((), (), s32[]{:S(2)}) async-start(), calls=%async_computation.1 | async-start | bytes 19660800 | tf_op jit(solution)/shard_map/all_gather | solution.py:91
  14.7 9.1 %copy-start.9 = (s32[32,4]{0,1:T(4,128)S(1)}, s32[32,4]{0,1:T(4,128)}, u32[]{:S(2)}) copy-start(s32[32,4]{0,1:T(4,128)} %param.26) | copy-start | bytes 1540
  14.7 9.4 %copy-start.6 = (s32[32,24,1]{0,2,1:T(1,128)S(1)}, s32[32,24,1]{0,2,1:T(1,128)}, u32[]{:S(2)}) copy-start(s32[32,24,1]{0,2,1:T(1,128)} %param.27) | copy-start | bytes 9220
  16.2 32.0 %all-to-all-start = ((bf16[32,2,64,1,256]{4,2,1,3,0:T(8,128)(2,1)}), bf16[32,2,64,1,256]{4,2,1,3,0:T(8,128)(2,1)}, u32[]{:S(2)}, u32[]{:S(2)}) async-start(bf16[32,2,64,1,256]{4,2,1,3,0:T(8,128)(2,1)} %broadcast_select_fusion), calls=%async_computation | async-start | bytes 4194304 | tf_op jit(solution)/shard_map/all_to_all | solution.py:143
  23.7 567.1 %all-gather.5.cloned.1.call-start = ((), (), s32[]{:S(2)}) async-start(), calls=%async_computation.2 | async-start | bytes 25952256 | tf_op jit(solution)/shard_map/all_gather | solution.py:178
  55.1 106.8 %copy-start.12 = (f32[5120]{0:T(1024)S(1)}, f32[5120]{0:T(1024)}, u32[]{:S(2)}) copy-start(f32[5120]{0:T(1024)} %param.17) | copy-start | bytes 61444
  161.9 8.8 %copy-start.10 = (f32[128]{0:T(128)S(1)}, f32[128]{0:T(128)}, u32[]{:S(2)}) copy-start(f32[128]{0:T(128)} %param.21) | copy-start | bytes 1540
  196.9 6.9 %copy-start.11 = (f32[128]{0:T(128)S(1)}, f32[128]{0:T(128)}, u32[]{:S(2)}) copy-start(f32[128]{0:T(128)} %param.20) | copy-start | bytes 1540
  222.7 7.1 %copy-start.3 = (f32[24,64,128]{2,1,0:T(8,128)S(1)}, f32[24,64,128]{2,1,0:T(8,128)}, u32[]{:S(2)}) copy-start(f32[24,64,128]{2,1,0:T(8,128)} %pad_maximum_fusion.2) | copy-start | bytes 2359300
  222.7 7.1 %copy-start.4 = (f32[24,64,128]{2,1,0:T(8,128)S(1)}, f32[24,64,128]{2,1,0:T(8,128)}, u32[]{:S(2)}) copy-start(f32[24,64,128]{2,1,0:T(8,128)} %pad_maximum_fusion.3) | copy-start | bytes 2359300
  229.9 9.9 %copy-start.2 = (bf16[1536,1,256]{2,0,1:T(8,128)(2,1)S(1)}, bf16[1536,1,256]{2,0,1:T(8,128)(2,1)}, u32[]{:S(2)}) copy-start(bf16[1536,1,256]{2,0,1:T(8,128)(2,1)} %copy.106) | copy-start | bytes 2359300
  590.8 13.5 %copy-start.1 = (bf16[5120,1,256]{2,0,1:T(8,128)(2,1)S(1)}, bf16[5120,1,256]{2,0,1:T(8,128)(2,1)}, u32[]{:S(2)}) copy-start(bf16[5120,1,256]{2,0,1:T(8,128)(2,1)} %param.19) | copy-start | bytes 7864324
Sparse Core Ops, SparseCore 0:
  9.7 145.1 all-gather.2
  230.0 92.4 all-gather.4
where the time goes:
time: 618 us; the launch traced here: 611 us
  local copies, waits for them, and re-layouts  214 us (35%)
  waiting for transfers between devices  116 us (19%)
  other arithmetic  111 us (18%)
  loops' own time  76.6 us (12%)
  matrix products  71.4 us (12%)
  between operations  14.5 us (2%)
  starting transfers between devices  7.55 us (1%)
    all_gather x1, waiting for transfers between devices, per_device(): gathered = lax.all_gather(hidden_in, 'tp', axis=1, tiled=True)  99.8 us
    dynamic_slice x120, local copies, waits for them, and re-layouts, per_device(): lax.map(one_page, (page_index, query_pages, my_session, my_start, my_pref...  79 us
    another operation x1, loops' own time, per_device(): lax.map(one_page, (page_index, query_pages, my_session, my_start, my_pref...  76.6 us
    squeeze x24, local copies, waits for them, and re-layouts, one_page(): lax.dynamic_index_in_dim(fetched_pages, session, 0, keepdims=False)  26.3 us
    dot_general x1, matrix products, per_device(): jnp.dot(normalized_input, w_query, preferred_element_type=jnp.float32)  24.5 us
    dot_general x24, matrix products, attend(): jnp.einsum('hgqk,khd->qhgd', probs, key_rows[..., head_dim:], preferred_e...  19.2 us
    dot_general x24, matrix products, attend(): jnp.einsum('qhgd,khd->hgqk', grouped, key_rows[..., :head_dim], preferred...  19 us
    select_n x48, other arithmetic, one_page(): span_key_rows = jnp.take(fresh, span_ids, axis=0)  17.5 us
  transfers between devices with their start and end apart: 3, of which 2 were waited for; matrix products, arithmetic and copies ran while one was open for 50% of the time, Pallas kernels for 0%

commit v1 on v0

v1 whole, which is shorter than its diff:
```python
import functools

import jax
import jax.numpy as jnp
from jax import lax
from jax.experimental import pallas as pl
from jax.experimental.pallas import tpu as pltpu
from jax.sharding import PartitionSpec as P

CHUNK_PAGES = (10, 8, 6)
KEY_BLOCK = 256
VMEM_BYTES = 56 * 1024 * 1024
LOG2E = 1.4426950408889634


def rotary_tables(positions, head_dim):
    half_dim = head_dim // 2
    exponent = jnp.arange(half_dim, dtype=jnp.float32) * (2.0 / head_dim)
    inverse = jnp.power(jnp.float32(1000000.0), -exponent)
    angles = positions.astype(jnp.float32)[:, None] * inverse[None, :]
    cosine, sine = jnp.cos(angles), jnp.sin(angles)
    return jnp.concatenate([cosine, cosine], -1), jnp.concatenate([-sine, sine], -1)


def page_layout(span_counts, prefix_counts, page_count):
    ends = jnp.cumsum(span_counts, axis=0)
    starts = ends - span_counts
    page_index = jnp.arange(page_count, dtype=jnp.int32)
    session_of = jnp.sum((page_index[:, None] >= ends[None, :]).astype(jnp.int32), -1)
    onehot = session_of[:, None] == jnp.arange(span_counts.shape[0], dtype=jnp.int32)
    start_of = jnp.sum(jnp.where(onehot, starts[None, :], 0), -1)
    prefix_of = jnp.sum(jnp.where(onehot, prefix_counts[None, :], 0), -1)
    return session_of, start_of, prefix_of


def target_ranks(targets):
    count = targets.shape[1]
    order = jnp.arange(count, dtype=jnp.int32)
    earlier = (targets[:, :, None] == targets[:, None, :]) & (
        order[None, None, :] < order[None, :, None]
    )
    return jnp.sum(earlier.astype(jnp.int32), -1)


def head_norm_rotary(values, gain, cosine, sine):
    mean_square = jnp.mean(values * values, axis=-1, keepdims=True)
    scaled = values * lax.rsqrt(mean_square + 1e-06) * gain
    return scaled * cosine + pltpu.roll(scaled, values.shape[-1] // 2, axis=1) * sine


def norm_kv_kernel(
    me_ref, own, left, right, far_top, far_low, gain, weight, k_gain, cosine, sine, normed, kv
):
    rows, width = own.shape
    me = me_ref[0]
    half = rows // 2
    tile = 16
    places = [pl.multiple_of(lax.rem(me + shift, 4) * width, 128) for shift in (0, 3, 1, 2)]

    def normalize(start, far, far_start):
        pieces = [
            own[pl.ds(start, tile), :],
            left[pl.ds(start, tile), :],
            right[pl.ds(start, tile), :],
            far[pl.ds(far_start, tile), :],
        ]
        total = jnp.zeros((tile, 128), jnp.float32)
        for piece in pieces:
            wide = piece.astype(jnp.float32)
            square = wide * wide
            for lane in range(0, width, 128):
                total = total + square[:, lane : lane + 128]
        mean_square = jnp.sum(total, axis=-1, keepdims=True) * (1.0 / (4 * width))
        scale = lax.rsqrt(mean_square + 1e-06)
        for piece, place in zip(pieces, places):
            scaled = piece.astype(jnp.float32) * scale * gain[:, pl.ds(place, width)]
            normed[pl.ds(start, tile), pl.ds(place, width)] = scaled.astype(jnp.bfloat16)

    @pl.loop(0, half // tile)
    def _(step):
        start = pl.multiple_of(step * tile, tile)
        normalize(start, far_top, start)

    @pl.loop(0, half // tile)
    def _(step):
        start = pl.multiple_of(step * tile, tile)
        normalize(pl.multiple_of(half + start, tile), far_low, start)

    head_dim = k_gain.shape[1]
    keyval = jnp.dot(normed[...], weight[...], preferred_element_type=jnp.float32)
    key = head_norm_rotary(keyval[:, :head_dim], k_gain[...], cosine[...], sine[...])
    kv[:, :head_dim] = key.astype(jnp.bfloat16)
    kv[:, head_dim:] = keyval[:, head_dim:].astype(jnp.bfloat16)


def norm_kv(me, pieces, gain, weight, k_gain, cosine, sine):
    rows, width = pieces[0].shape
    return pl.pallas_call(
        norm_kv_kernel,
        out_shape=(
            jax.ShapeDtypeStruct((rows, 4 * width), jnp.bfloat16),
            jax.ShapeDtypeStruct((rows, weight.shape[1]), jnp.bfloat16),
        ),
        in_specs=[pl.BlockSpec(memory_space=pltpu.SMEM)]
        + [pl.BlockSpec(memory_space=pltpu.VMEM)] * 10,
        out_specs=[pl.BlockSpec(memory_space=pltpu.VMEM)] * 2,
        compiler_params=pltpu.CompilerParams(vmem_limit_bytes=VMEM_BYTES),
        cost_estimate=pl.CostEstimate(
            flops=2 * rows * 4 * width * weight.shape[1],
            bytes_accessed=16 * rows * width + 8 * width * weight.shape[1],
            transcendentals=0,
        ),
        name="norm_kv",
    )(me, *pieces, gain, weight, k_gain, cosine, sine)


def query_kernel(normed, weight, q_gain, cosine, sine, query):
    head_dim = q_gain.shape[1]
    product = jnp.dot(normed[...], weight[...], preferred_element_type=jnp.float32)
    for start in range(0, product.shape[1], head_dim):
        rotated = head_norm_rotary(
            product[:, start : start + head_dim], q_gain[...], cosine[...], sine[...]
        )
        query[:, start : start + head_dim] = rotated.astype(jnp.bfloat16)


def project_query(normed, weight, q_gain, cosine, sine):
    rows, depth = normed.shape
    columns = weight.shape[1]
    tile = 256
    whole = lambda shape: pl.BlockSpec(shape, lambda n: (0, 0))
    return pl.pallas_call(
        query_kernel,
        grid=(columns // tile,),
        out_shape=jax.ShapeDtypeStruct((rows, columns), jnp.bfloat16),
        in_specs=[
            whole((rows, depth)),
            pl.BlockSpec((depth, tile), lambda n: (0, n)),
            whole(q_gain.shape),
            whole(cosine.shape),
            whole(sine.shape),
        ],
        out_specs=pl.BlockSpec((rows, tile), lambda n: (0, n)),
        compiler_params=pltpu.CompilerParams(vmem_limit_bytes=VMEM_BYTES),
        cost_estimate=pl.CostEstimate(
            flops=2 * rows * depth * columns,
            bytes_accessed=2 * (rows * depth + depth * columns + rows * columns),
            transcendentals=0,
        ),
        name="query",
    )(normed, weight, q_gain, cosine, sine)


def attention_kernel(
    page_base, chunk_count, session, start, prefix, query, prefix_kv, *refs
):
    kv_chunks = refs[:chunk_count]
    out, span = refs[-2:]
    step = pl.program_id(0)
    page = page_base + step
    head_dim = prefix_kv.shape[1] // 2
    page_size = query.shape[0]
    heads = query.shape[1] // head_dim
    rows = heads * page_size
    block_pages = KEY_BLOCK // page_size

    @pl.when(step == 0)
    def _():
        filled = 0
        for chunk in kv_chunks:
            span[pl.ds(filled, chunk.shape[0]), :] = chunk[...]
            filled += chunk.shape[0]
        if filled < span.shape[0]:
            span[filled:, :] = jnp.zeros((span.shape[0] - filled, span.shape[1]), span.dtype)

    grouped = jnp.concatenate(
        [query[:, h * head_dim : (h + 1) * head_dim] for h in range(heads)], axis=0
    )
    factor = LOG2E / float(head_dim) ** 0.5
    my_prefix = prefix[page]
    my_start = start[page]
    prefix_base = session[page] * (prefix_kv.shape[0] // 4)
    column = lax.broadcasted_iota(jnp.int32, (rows, KEY_BLOCK), 1)
    token = lax.broadcasted_iota(jnp.int32, (rows, KEY_BLOCK), 0) & (page_size - 1)

    def update(carry, keys_values, visible):
        top, total, mixed = carry
        scores = lax.dot_general(
            grouped,
            keys_values[:, :head_dim],
            (((1,), (1,)), ((), ())),
            preferred_element_type=jnp.float32,
        )
        scores = jnp.where(visible, scores * factor, -jnp.inf)
        new_top = jnp.maximum(top, jnp.max(scores, axis=-1, keepdims=True))
        weights = jnp.exp2(scores - new_top)
        fade = jnp.exp2(top - new_top)
        total = total * fade + jnp.sum(weights, axis=-1, keepdims=True)
        mixed = mixed * fade + jnp.dot(
            weights.astype(jnp.bfloat16),
            keys_values[:, head_dim:],
            preferred_element_type=jnp.float32,
        )
        return new_top, total, mixed

    def prefix_block(block, carry):
        base = pl.multiple_of(block * KEY_BLOCK, KEY_BLOCK)
        rows_at = pl.multiple_of(prefix_base + base, KEY_BLOCK)
        visible = column < my_prefix * page_size - base
        return update(carry, prefix_kv[pl.ds(rows_at, KEY_BLOCK), :], visible)

    def span_block(block, carry):
        base = my_start * page_size + block * KEY_BLOCK
        rows_at = pl.multiple_of(jnp.minimum(base, span.shape[0] - KEY_BLOCK), page_size)
        absolute = column + rows_at
        visible = (absolute >= base) & (absolute <= page * page_size + token)
        return update(carry, span[pl.ds(rows_at, KEY_BLOCK), :], visible)

    carry = (
        jnp.full((rows, 1), -jnp.inf, jnp.float32),
        jnp.zeros((rows, 1), jnp.float32),
        jnp.zeros((rows, head_dim), jnp.float32),
    )
    carry = lax.fori_loop(
        0, lax.div(my_prefix + (block_pages - 1), block_pages), prefix_block, carry
    )
    span_count = lax.div(page - my_start + block_pages, block_pages)
    carry = lax.fori_loop(0, span_count, span_block, carry)
    mixed = (carry[2] / carry[1]).astype(jnp.bfloat16)
    for h in range(heads):
        out[:, h * head_dim : (h + 1) * head_dim] = mixed[h * page_size : (h + 1) * page_size]


def attention(page_base, layout, query, prefix_kv, kv_chunks, previous, row_count, page_size):
    rows, columns = query.shape
    pages = rows // page_size
    whole = lambda shape: pl.BlockSpec(shape, lambda p, *_: (0, 0))
    operands = [query, prefix_kv, *kv_chunks]
    in_specs = [pl.BlockSpec((page_size, columns), lambda p, *_: (p, 0))]
    in_specs += [whole(operand.shape) for operand in operands[1:]]
    aliases = {}
    if previous is not None:
        aliases = {len(layout) + len(operands): 0}
        operands.append(previous)
        in_specs.append(pl.BlockSpec(memory_space=pl.ANY))
    return pl.pallas_call(
        functools.partial(attention_kernel, page_base, len(kv_chunks)),
        grid_spec=pltpu.PrefetchScalarGridSpec(
            num_scalar_prefetch=len(layout),
            grid=(pages,),
            in_specs=in_specs,
            out_specs=pl.BlockSpec((page_size, columns), lambda p, *_: (page_base + p, 0)),
            scratch_shapes=[pltpu.VMEM((row_count, prefix_kv.shape[1]), jnp.bfloat16)],
        ),
        out_shape=jax.ShapeDtypeStruct((row_count, columns), jnp.bfloat16),
        input_output_aliases=aliases,
        compiler_params=pltpu.CompilerParams(vmem_limit_bytes=VMEM_BYTES),
        cost_estimate=pl.CostEstimate(
            flops=4 * rows * columns * 1200,
            bytes_accessed=4 * rows * columns + 6 * prefix_kv.size,
            transcendentals=rows * 8 * 1200,
        ),
        name="attention",
    )(*layout, *operands)


def per_device(
    hidden_in,
    ln_gain,
    w_query,
    key_value_weight,
    q_gain,
    k_gain,
    key_value_cache,
    prefix_pages,
    page_holder,
    page_slot,
    span_pages,
    decode_target,
):
    replica = lax.axis_index("rep")
    me = lax.axis_index("tp").astype(jnp.int32)
    replicas = lax.axis_size("rep")
    parts = lax.axis_size("tp")
    up = [(i, (i + 1) % parts) for i in range(parts)]
    down = [(i, (i - 1) % parts) for i in range(parts)]
    head_dim = q_gain.shape[0]
    page_size = key_value_cache.shape[1]
    row_count = hidden_in.shape[0]
    page_count = row_count // page_size
    sessions = span_pages.shape[1]
    max_pages = page_holder.shape[2]
    capacity = sessions * max_pages // replicas
    push_slots = 2

    pieces = []
    row = 0
    for pages in CHUNK_PAGES:
        rows = pages * page_size
        own = hidden_in[row : row + rows]
        left = lax.ppermute(own, "tp", up)
        right = lax.ppermute(own, "tp", down)
        pieces.append((own, left, right))
        row += rows
    chunks = []
    for own, left, right in pieces:
        half = own.shape[0] // 2
        far_top = lax.ppermute(left[:half], "tp", up)
        far_low = lax.ppermute(right[half:], "tp", down)
        chunks.append((own, left, right, far_top, far_low))

    position_count = sessions * max_pages
    flat_holder = page_holder.reshape(replicas, position_count)
    flat_slot = page_slot.reshape(replicas, position_count)
    from_here = flat_holder == replica
    send_rank = jnp.cumsum(from_here.astype(jnp.int32), axis=1) - 1
    slot_range = jnp.arange(capacity, dtype=jnp.int32)
    matched = from_here[:, None, :] & (send_rank[:, None, :] == slot_range[None, :, None])
    local_ids = jnp.sum(jnp.where(matched, flat_slot[:, None, :], 0), -1)
    cache = key_value_cache.reshape(-1, page_size, 2 * head_dim)
    outgoing = jnp.take(cache, local_ids.reshape(-1), axis=0, mode="clip")
    outgoing = outgoing.reshape(replicas, capacity, page_size, 2 * head_dim)
    incoming = lax.all_to_all(outgoing, "rep", split_axis=0, concat_axis=0, tiled=True)
    incoming = incoming.reshape(replicas * capacity, page_size, 2 * head_dim)
    my_holder = lax.dynamic_index_in_dim(flat_holder, replica, 0, keepdims=False)
    position_index = jnp.arange(position_count, dtype=jnp.int32)
    same_earlier = (my_holder[:, None] == my_holder[None, :]) & (
        position_index[None, :] < position_index[:, None]
    )
    recv_rank = jnp.sum(same_earlier.astype(jnp.int32), axis=1)
    recv_ids = my_holder * capacity + recv_rank
    prefix_kv = jnp.take(incoming, recv_ids, axis=0, mode="clip")
    prefix_kv = prefix_kv.reshape(position_count * page_size, 2 * head_dim)

    my_span = lax.dynamic_index_in_dim(span_pages, replica, 0, keepdims=False)
    my_prefix = lax.dynamic_index_in_dim(prefix_pages, replica, 0, keepdims=False)
    layout = page_layout(my_span, my_prefix, page_count)
    session_of, start_of, prefix_of = layout
    page_index = jnp.arange(page_count, dtype=jnp.int32)
    page_first = (prefix_of + page_index - start_of) * page_size
    positions = (page_first[:, None] + jnp.arange(page_size, dtype=jnp.int32)[None, :]).reshape(-1)
    cosine, sine = rotary_tables(positions, head_dim)

    targets = decode_target[..., 0]
    my_targets = lax.dynamic_index_in_dim(targets, replica, 0, keepdims=True)
    my_ranks = target_ranks(my_targets)[0]
    wanted = jnp.arange(replicas * push_slots, dtype=jnp.int32)
    chosen = (my_targets[0] * push_slots + my_ranks)[None, :] == wanted[:, None]
    push_ids = jnp.sum(jnp.where(chosen, page_index[None, :], 0), -1)
    push_valid = jnp.any(chosen, axis=-1)

    gain = ln_gain.reshape(1, -1)
    kv_weight = key_value_weight.reshape(key_value_weight.shape[0], -1)
    q_gain, k_gain = q_gain.reshape(1, -1), k_gain.reshape(1, -1)
    kv_chunks = []
    attn_out = None
    row = 0
    for index, chunk in enumerate(chunks):
        rows = chunk[0].shape[0]
        cos_rows, sin_rows = cosine[row : row + rows], sine[row : row + rows]
        normed, kv = norm_kv(me[None], chunk, gain, kv_weight, k_gain, cos_rows, sin_rows)
        kv_chunks.append(kv)
        if index == len(chunks) - 1:
            fresh = jnp.concatenate(kv_chunks, 0).reshape(page_count, page_size, 2 * head_dim)
            pushing = jnp.take(fresh, push_ids, axis=0, mode="clip")
            pushing = jnp.where(push_valid[:, None, None], pushing, jnp.zeros_like(pushing))
            pushing = pushing.reshape(replicas, push_slots, page_size, 2 * head_dim)
            pushed = lax.all_to_all(pushing, "rep", split_axis=0, concat_axis=0, tiled=True)
        query = project_query(normed, w_query, q_gain, cos_rows, sin_rows)
        attn_out = attention(
            row // page_size, layout, query, prefix_kv, kv_chunks, attn_out, row_count, page_size
        )
        row += rows
    pushed = pushed.reshape(replicas * push_slots, page_size, 1, 2 * head_dim)
    return (attn_out, pushed)


def solution(mesh):
    placed = (
        P("rep", "tp"),
        P(),
        P(None, "tp"),
        P(None, "tp", None),
        P(),
        P(),
        P("rep", None, "tp", None),
        P(),
        P(),
        P(),
        P(),
        P(),
    )
    return jax.shard_map(
        per_device,
        mesh=mesh,
        in_specs=placed,
        out_specs=(P("rep", "tp"), P("rep", None, "tp", None)),
        check_vma=False,
    )
```

time: 618 us -> 336 us (0.54)
  local copies, waits for them, and re-layouts: 214 us -> 29.5 us
  Pallas kernels: 0 us -> 164 us
  other arithmetic: 111 us -> 11.9 us
  loops' own time: 76.6 us -> 0 us
  matrix products: 71.4 us -> 0 us
  starting transfers between devices: 7.55 us -> 30 us
  waiting for transfers between devices: 116 us -> 96.2 us
  between operations: 14.5 us -> 0.88 us
    pallas_call x0 -> x9, Pallas kernels: none -> 164 us  [the longest x3 90.2 us: attention(): pl.pallas_call(functools.partial(attention_kernel, page_base, len(kv_chun...]
    all_gather x2 -> x0, waiting for transfers between devices: 99.8 us -> none  [the longest x1 99.8 us: per_device(): gathered = lax.all_gather(hidden_in, 'tp', axis=1, tiled=True)]
    ppermute x0 -> x12, waiting for transfers between devices: none -> 96.2 us  [the longest x3 62.4 us: per_device(): left = lax.ppermute(own, 'tp', up)]
    dynamic_slice x124 -> x2, local copies, waits for them, and re-layouts: 79.7 us -> 0.78 us  [the longest x1 0.59 us: per_device(): my_targets = lax.dynamic_index_in_dim(targets, replica, 0, keepdims=True)]
    another operation x1 -> x0, loops' own time: 76.6 us -> none  [per_device(): lax.map(one_page, (page_index, query_pages, my_session, my_start, my_pref...]
    dot_general x50 -> x0, matrix products: 71.4 us -> none  [the longest x1 24.5 us: per_device(): jnp.dot(normalized_input, w_query, preferred_element_type=jnp.float32)]
    squeeze x24 -> x0, local copies, waits for them, and re-layouts: 26.3 us -> none  [one_page(): lax.dynamic_index_in_dim(fetched_pages, session, 0, keepdims=False)]
    gather x27 -> x3, local copies, waits for them, and re-layouts: 31.2 us -> 6.27 us  [the longest x1 3.59 us: per_device(): prefix_kv = jnp.take(incoming, recv_ids, axis=0, mode='clip')]
  transfers between devices with their start and end apart: 3 -> 14, of which waited for: 2 -> 4; matrix products, arithmetic and copies ran while one was open for 50% -> 10% of each run, Pallas kernels for 0% -> 49%
where the time goes in v1:
time: 336 us; the launch traced here: 332 us
  Pallas kernels  164 us (49%)
  waiting for transfers between devices  96.2 us (29%)
  starting transfers between devices  30 us (9%)
  local copies, waits for them, and re-layouts  29.5 us (9%)
  other arithmetic  11.9 us (4%)
    pallas_call x3, Pallas kernels, attention(): pl.pallas_call(functools.partial(attention_kernel, page_base, len(kv_chun...  90.2 us
    ppermute x3, waiting for transfers between devices, per_device(): left = lax.ppermute(own, 'tp', up)  62.4 us
    pallas_call x3, Pallas kernels, project_query(): pl.pallas_call(query_kernel, grid=(columns // tile,), out_shape=jax.Shape...  40.3 us
    pallas_call x3, Pallas kernels, norm_kv(): pl.pallas_call(norm_kv_kernel, out_shape=(jax.ShapeDtypeStruct((rows, 4 *...  33.4 us
    ppermute x3, waiting for transfers between devices, per_device(): far_low = lax.ppermute(right[half:], 'tp', down)  22.4 us
    ppermute x3, waiting for transfers between devices, per_device(): right = lax.ppermute(own, 'tp', down)  11.5 us
    all_to_all x1, starting transfers between devices, per_device(): lax.all_to_all(pushing, 'rep', split_axis=0, concat_axis=0, tiled=True)  10.2 us
    all_to_all x1, starting transfers between devices, per_device(): lax.all_to_all(outgoing, 'rep', split_axis=0, concat_axis=0, tiled=True)  8.88 us
  transfers between devices with their start and end apart: 14, of which 4 were waited for; matrix products, arithmetic and copies ran while one was open for 10% of the time, Pallas kernels for 49%

profile of v1, /device:TPU:125, one launch (start us, length us, event | category | flops | bytes accessed | tf_op | source)
XLA Modules:
  0.0 332.5 jit_solution(15482608390746435526)
XLA Ops:
  0.6 2.8 slice.50.own
  5.0 2.5 slice.55.own
  8.9 2.2 slice.45.own
  11.1 2.5 collective-permute-start
  16.4 8.9 %all-to-all-start = ((bf16[32,2,64,256]{3,2,1,0:T(8,128)(2,1)}), bf16[32,2,64,256]{3,2,1,0:T(8,128)(2,1)}, u32[]{:S(2)}, u32[]{:S(2)}) async-start(bf16[32,2,64,256]{3,2,1,0:T(8,128)(2,1)} %bitcast.41), calls=%async_computation | async-start | bytes 4194304 | tf_op jit(solution)/shard_map/all_to_all | solution.py:323
  27.2 62.4 %collective-permute-done.left = bf16[384,1280]{1,0:T(8,128)(2,1)S(1)} collective-permute-done((bf16[384,1280]{1,0:T(8,128)(2,1)}, bf16[384,1280]{1,0:T(8,128)(2,1)S(1)}, u32[]{:S(2)}, u32[]{:S(2)}) %collective-permute-start) | collective-permute-done | bytes 983072 | tf_op jit(solution)/shard_map/ppermute | solution.py:301
  91.0 2.8 fusion
  94.7 2.3 collective-permute-start.2
  102.2 11.5 %collective-permute-done.1.right = bf16[384,1280]{1,0:T(8,128)(2,1)S(1)} collective-permute-done((bf16[384,1280]{1,0:T(8,128)(2,1)}, bf16[384,1280]{1,0:T(8,128)(2,1)S(1)}, u32[]{:S(2)}, u32[]{:S(2)}) %collective-permute-start.1) | collective-permute-done | bytes 983072 | tf_op jit(solution)/shard_map/ppermute | solution.py:302
  117.4 2.7 collective-permute-start.10
  125.7 17.2 %collective-permute-done.3.far_low = bf16[192,1280]{1,0:T(8,128)(2,1)} collective-permute-done((bf16[192,1280]{1,0:T(8,128)(2,1)}, bf16[192,1280]{1,0:T(8,128)(2,1)}, u32[]{:S(2)}, u32[]{:S(2)}) %collective-permute-start.3) | collective-permute-done | bytes 491552 | tf_op jit(solution)/shard_map/ppermute | solution.py:309
  143.0 8.9 %norm_kv.3 = (bf16[384,5120]{1,0:T(8,128)(2,1)}, bf16[384,256]{1,0:T(8,128)(2,1)}) custom-call(s32[1]{0:T(128)} %bitcast.4.me_ref, bf16[384,1280]{1,0:T(8,128)(2,1)} %slice.45.own, bf16[384,1280]{1,0:T(8,128)(2,1)} %copy-done.3, bf16[384,1280]{1,0:T(8,128)(2,1)} %copy-done.5, bf16[192,1280]{1,0:T(8,128)(2,1)} %copy-done.8, ...), custom_call_target="tpu_custom_call" | custom-call | flops 1006632960 | bytes 10485760 | tf_op jit(solution)/shard_map/norm_kv/pallas_call | solution.py:98
  151.9 5.2 %collective-permute-done.11.far_low = bf16[256,1280]{1,0:T(8,128)(2,1)} collective-permute-done((bf16[256,1280]{1,0:T(8,128)(2,1)}, bf16[256,1280]{1,0:T(8,128)(2,1)}, u32[]{:S(2)}, u32[]{:S(2)}) %collective-permute-start.11) | collective-permute-done | bytes 655392 | tf_op jit(solution)/shard_map/ppermute | solution.py:309
  157.0 11.1 %norm_kv.5 = (bf16[512,5120]{1,0:T(8,128)(2,1)}, bf16[512,256]{1,0:T(8,128)(2,1)}) custom-call(s32[1]{0:T(128)} %bitcast.4.me_ref, bf16[512,1280]{1,0:T(8,128)(2,1)} %slice.55.own, bf16[512,1280]{1,0:T(8,128)(2,1)} %collective-permute-done.8.left, bf16[512,1280]{1,0:T(8,128)(2,1)} %collective-permute-done.9.right, bf16[256,1280]{1,0:T(8,128)(2,1)} %copy-done.7, ...), custom_call_target="tpu_custom_call" | custom-call | flops 1342177280 | bytes 13107200 | tf_op jit(solution)/shard_map/norm_kv/pallas_call | solution.py:98
  168.2 13.4 %norm_kv.4 = (bf16[640,5120]{1,0:T(8,128)(2,1)}, bf16[640,256]{1,0:T(8,128)(2,1)}) custom-call(s32[1]{0:T(128)} %bitcast.4.me_ref, bf16[640,1280]{1,0:T(8,128)(2,1)} %slice.50.own, bf16[640,1280]{1,0:T(8,128)(2,1)} %collective-permute-done.4.left, bf16[640,1280]{1,0:T(8,128)(2,1)} %collective-permute-done.5.right, ...), custom_call_target="tpu_custom_call" | custom-call | flops 1677721600 | bytes 15728640 | tf_op jit(solution)/shard_map/norm_kv/pallas_call | solution.py:98
  184.8 10.2 %all-to-all-start.1 = ((bf16[32,2,64,256]{3,2,1,0:T(8,128)(2,1)}), bf16[32,2,64,256]{3,2,1,0:T(8,128)(2,1)}, u32[]{:S(2)}, u32[]{:S(2)}) async-start(bf16[32,2,64,256]{3,2,1,0:T(8,128)(2,1)} %broadcast_select_fusion), calls=%async_computation.1 | async-start | bytes 4194304 | tf_op jit(solution)/shard_map/all_to_all | solution.py:368
  195.0 10.2 %query.3 = bf16[384,1024]{1,0:T(8,128)(2,1)} custom-call(bf16[384,5120]{1,0:T(8,128)(2,1)} %get-tuple-element.8.normed, bf16[5120,1024]{1,0:T(8,128)(2,1)} %weight.5, f32[1,128]{1,0:T(1,128)} %bitcast.50, f32[384,128]{1,0:T(8,128)} %pad_maximum_fusion.6.cosine, f32[384,128]{1,0:T(8,128)} %pad_maximum_fusion.5.sine), custom_call_target="tpu_custom_call" | custom-call | flops 4026531840 | bytes 15204352 | tf_op jit(solution)/shard_map/query/pallas_call | solution.py:132
  205.3 13.3 %query.4 = bf16[512,1024]{1,0:T(8,128)(2,1)} custom-call(bf16[512,5120]{1,0:T(8,128)(2,1)} %get-tuple-element.12.normed, bf16[5120,1024]{1,0:T(8,128)(2,1)} %weight.5, f32[1,128]{1,0:T(1,128)} %bitcast.51, f32[512,128]{1,0:T(8,128)} %pad_maximum_fusion.4.cosine, f32[512,128]{1,0:T(8,128)} %pad_maximum_fusion.3.sine), custom_call_target="tpu_custom_call" | custom-call | flops 5368709120 | bytes 16777216 | tf_op jit(solution)/shard_map/query/pallas_call | solution.py:132
  218.6 3.6 %gather_fusion.1 = bf16[64,64,256]{2,1,0:T(8,128)(2,1)} fusion(bf16[64,64,256]{2,1,0:T(8,128)(2,1)} %bitcast.13, s32[1024]{0:T(1024)S(1)} %pad_clamp_fusion.1), kind=kCustom, calls=%fused_computation.1 | custom fusion | bytes 4194560 | tf_op jit(solution)/shard_map/jit(_take)/gather | solution.py:332
  222.2 16.8 %query.5 = bf16[640,1024]{1,0:T(8,128)(2,1)} custom-call(bf16[640,5120]{1,0:T(8,128)(2,1)} %get-tuple-element.13.normed, bf16[5120,1024]{1,0:T(8,128)(2,1)} %weight.5, f32[1,128]{1,0:T(1,128)} %bitcast.52, f32[640,128]{1,0:T(8,128)} %pad_maximum_fusion.2.cosine, f32[640,128]{1,0:T(8,128)} %pad_maximum_fusion.1.sine), custom_call_target="tpu_custom_call" | custom-call | flops 6710886400 | bytes 18350080 | tf_op jit(solution)/shard_map/query/pallas_call | solution.py:132
  238.9 35.8 %attention.3.refs_2_ = bf16[1536,1024]{1,0:T(8,128)(2,1)} custom-call(s32[24]{0:T(128)} %copy-done.12, s32[24]{0:T(128)} %copy-done.14, s32[24]{0:T(128)} %copy-done.13, bf16[640,1024]{1,0:T(8,128)(2,1)} %query.5, bf16[4096,256]{1,0:T(8,128)(2,1)} %bitcast.36, bf16[640,256]{1,0:T(8,128)(2,1)} %get-tuple-element.9.refs_0_), custom_call_target="tpu_custom_call" | custom-call | flops 3145728000 | bytes 8912896 | tf_op jit(solution)/shard_map/attention/pallas_call | solution.py:246
  274.7 27.0 %attention.4.refs_3_ = bf16[1536,1024]{1,0:T(8,128)(2,1)} custom-call(s32[24]{0:T(128)} %copy-done.12, s32[24]{0:T(128)} %copy-done.14, s32[24]{0:T(128)} %copy-done.13, bf16[512,1024]{1,0:T(8,128)(2,1)} %query.4, bf16[4096,256]{1,0:T(8,128)(2,1)} %bitcast.37, bf16[640,256]{1,0:T(8,128)(2,1)} %get-tuple-element.9.refs_0_, ...), custom_call_target="tpu_custom_call", output_to_operand_aliasing={{}: (7, {})} | custom-call | flops 2516582400 | bytes 8388608 | tf_op jit(solution)/shard_map/attention/pallas_call | solution.py:246
  301.7 27.4 %attention.5 = bf16[1536,1024]{1,0:T(8,128)(2,1)} custom-call(s32[24]{0:T(128)} %copy-done.12, s32[24]{0:T(128)} %copy-done.14, s32[24]{0:T(128)} %copy-done.13, bf16[384,1024]{1,0:T(8,128)(2,1)} %query.3, bf16[4096,256]{1,0:T(8,128)(2,1)} %bitcast.38, bf16[640,256]{1,0:T(8,128)(2,1)} %get-tuple-element.9.refs_0_, ...), custom_call_target="tpu_custom_call", output_to_operand_aliasing={{}: (8, {})} | custom-call | flops 1887436800 | bytes 7864320 | tf_op jit(solution)/shard_map/attention/pallas_call | solution.py:246
  329.2 3.3 copy.33
  (99 shorter events, 27.7 us)
Async XLA Ops:
  0.6 13.7 %copy-start = (bf16[64,64,1,256]{3,1,2,0:T(8,128)(2,1)S(1)}, bf16[64,64,1,256]{3,1,2,0:T(8,128)(2,1)}, u32[]{:S(2)}) copy-start(bf16[64,64,1,256]{3,1,2,0:T(8,128)(2,1)} %param.18) | copy-start | bytes 6291460
  3.5 10.1 %copy-start.9 = (s32[32,4,16]{0,2,1:T(8,128)S(1)}, s32[32,4,16]{0,2,1:T(8,128)}, u32[]{:S(2)}) copy-start(s32[32,4,16]{0,2,1:T(8,128)} %param.21) | copy-start | bytes 24580
  3.5 10.2 %copy-start.10 = (s32[32,4,16]{0,2,1:T(8,128)S(1)}, s32[32,4,16]{0,2,1:T(8,128)}, u32[]{:S(2)}) copy-start(s32[32,4,16]{0,2,1:T(8,128)} %param.20) | copy-start | bytes 24580
  3.5 91.2 %collective-permute-start.4 = (bf16[640,1280]{1,0:T(8,128)(2,1)}, bf16[640,1280]{1,0:T(8,128)(2,1)}, u32[]{:S(2)}, u32[]{:S(2)}) collective-permute-start(bf16[640,1280]{1,0:T(8,128)(2,1)} %slice.50.own), channel_id=1, source_target_pairs={{0,1},{1,2},{2,3},{3,0},{4,5},{5,6},{6,7},{7,4},{8,9},{9,10},{10,1... | collective-permute-start | bytes 4915208 | tf_op jit(solution)/shard_map/ppermute | solution.py:301
  3.5 96.5 %collective-permute-start.5 = (bf16[640,1280]{1,0:T(8,128)(2,1)}, bf16[640,1280]{1,0:T(8,128)(2,1)}, u32[]{:S(2)}, u32[]{:S(2)}) collective-permute-start(bf16[640,1280]{1,0:T(8,128)(2,1)} %slice.50.own), channel_id=1, source_target_pairs={{0,3},{1,0},{2,1},{3,2},{4,7},{5,4},{6,5},{7,6},{8,11},{9,8},{10,9... | collective-permute-start | bytes 4915208 | tf_op jit(solution)/shard_map/ppermute | solution.py:302
  7.4 108.0 %collective-permute-start.8 = (bf16[512,1280]{1,0:T(8,128)(2,1)}, bf16[512,1280]{1,0:T(8,128)(2,1)}, u32[]{:S(2)}, u32[]{:S(2)}) collective-permute-start(bf16[512,1280]{1,0:T(8,128)(2,1)} %slice.55.own), channel_id=1, source_target_pairs={{0,1},{1,2},{2,3},{3,0},{4,5},{5,6},{6,7},{7,4},{8,9},{9,10},{10,1... | collective-permute-start | bytes 3932168 | tf_op jit(solution)/shard_map/ppermute | solution.py:301
  8.7 108.7 %collective-permute-start.9 = (bf16[512,1280]{1,0:T(8,128)(2,1)}, bf16[512,1280]{1,0:T(8,128)(2,1)}, u32[]{:S(2)}, u32[]{:S(2)}) collective-permute-start(bf16[512,1280]{1,0:T(8,128)(2,1)} %slice.55.own), channel_id=1, source_target_pairs={{0,3},{1,0},{2,1},{3,2},{4,7},{5,4},{6,5},{7,6},{8,11},{9,8},{10,9... | collective-permute-start | bytes 3932168 | tf_op jit(solution)/shard_map/ppermute | solution.py:302
  11.1 78.4 %collective-permute-start = (bf16[384,1280]{1,0:T(8,128)(2,1)}, bf16[384,1280]{1,0:T(8,128)(2,1)S(1)}, u32[]{:S(2)}, u32[]{:S(2)}) collective-permute-start(bf16[384,1280]{1,0:T(8,128)(2,1)} %slice.45.own), channel_id=1, source_target_pairs={{0,1},{1,2},{2,3},{3,0},{4,5},{5,6},{6,7},{7,4},{8,9},{9,10},{10,1... | collective-permute-start | bytes 2949128 | tf_op jit(solution)/shard_map/ppermute | solution.py:301
  16.4 8.9 %copy-start.16 = (s32[32,4]{0,1:T(4,128)S(1)}, s32[32,4]{0,1:T(4,128)}, u32[]{:S(2)}) copy-start(s32[32,4]{0,1:T(4,128)} %param.22) | copy-start | bytes 1540
  16.4 9.7 %copy-start.11 = (s32[32,24,1]{0,2,1:T(1,128)S(1)}, s32[32,24,1]{0,2,1:T(1,128)}, u32[]{:S(2)}) copy-start(s32[32,24,1]{0,2,1:T(1,128)} %param.23) | copy-start | bytes 9220
  16.4 168.5 %all-to-all-start = ((bf16[32,2,64,256]{3,2,1,0:T(8,128)(2,1)}), bf16[32,2,64,256]{3,2,1,0:T(8,128)(2,1)}, u32[]{:S(2)}, u32[]{:S(2)}) async-start(bf16[32,2,64,256]{3,2,1,0:T(8,128)(2,1)} %bitcast.41), calls=%async_computation | async-start | bytes 4194304 | tf_op jit(solution)/shard_map/all_to_all | solution.py:323
  25.8 68.8 %copy-start.12 = (s32[24]{0:T(128)}, s32[24]{0:T(128)S(1)}, u32[]{:S(2)}) copy-start(s32[24]{0:T(128)S(1)} %convert_reduce_fusion.2.session) | copy-start | bytes 292
  25.9 68.7 %copy-start.13 = (s32[24]{0:T(128)}, s32[24]{0:T(128)S(1)}, u32[]{:S(2)}) copy-start(s32[24]{0:T(128)S(1)} %get-tuple-element.14.prefix) | copy-start | bytes 292
  25.9 68.7 %copy-start.14 = (s32[24]{0:T(128)}, s32[24]{0:T(128)S(1)}, u32[]{:S(2)}) copy-start(s32[24]{0:T(128)S(1)} %get-tuple-element.15.start) | copy-start | bytes 292
  90.5 23.1 %collective-permute-start.1 = (bf16[384,1280]{1,0:T(8,128)(2,1)}, bf16[384,1280]{1,0:T(8,128)(2,1)S(1)}, u32[]{:S(2)}, u32[]{:S(2)}) collective-permute-start(bf16[384,1280]{1,0:T(8,128)(2,1)} %slice.45.own), channel_id=1, source_target_pairs={{0,3},{1,0},{2,1},{3,2},{4,7},{5,4},{6,5},{7,6},{8,11},{9,8},{10,9... | collective-permute-start | bytes 2949128 | tf_op jit(solution)/shard_map/ppermute | solution.py:302
  94.7 27.4 %collective-permute-start.2 = (bf16[192,1280]{1,0:T(8,128)(2,1)S(1)}, bf16[192,1280]{1,0:T(8,128)(2,1)S(1)}, u32[]{:S(2)}, u32[]{:S(2)}) collective-permute-start(bf16[192,1280]{1,0:T(8,128)(2,1)S(1)} %slice.66), channel_id=1, source_target_pairs={{0,1},{1,2},{2,3},{3,0},{4,5},{5,6},{6,7},{7,4},{8,9},{9,10},{10,1... | collective-permute-start | bytes 1474568 | tf_op jit(solution)/shard_map/ppermute | solution.py:308
  100.0 68.2 %collective-permute-start.6 = (bf16[320,1280]{1,0:T(8,128)(2,1)}, bf16[320,1280]{1,0:T(8,128)(2,1)}, u32[]{:S(2)}, u32[]{:S(2)}) collective-permute-start(bf16[320,1280]{1,0:T(8,128)(2,1)} %slice.68), channel_id=1, source_target_pairs={{0,1},{1,2},{2,3},{3,0},{4,5},{5,6},{6,7},{7,4},{8,9},{9,10},{10,1... | collective-permute-start | bytes 2457608 | tf_op jit(solution)/shard_map/ppermute | solution.py:308
  113.6 54.5 %collective-permute-start.7 = (bf16[320,1280]{1,0:T(8,128)(2,1)}, bf16[320,1280]{1,0:T(8,128)(2,1)}, u32[]{:S(2)}, u32[]{:S(2)}) collective-permute-start(bf16[320,1280]{1,0:T(8,128)(2,1)} %slice.69), channel_id=1, source_target_pairs={{0,3},{1,0},{2,1},{3,2},{4,7},{5,4},{6,5},{7,6},{8,11},{9,8},{10,9... | collective-permute-start | bytes 2457608 | tf_op jit(solution)/shard_map/ppermute | solution.py:309
  115.4 27.5 %collective-permute-start.3 = (bf16[192,1280]{1,0:T(8,128)(2,1)}, bf16[192,1280]{1,0:T(8,128)(2,1)}, u32[]{:S(2)}, u32[]{:S(2)}) collective-permute-start(bf16[192,1280]{1,0:T(8,128)(2,1)} %slice.67), channel_id=1, source_target_pairs={{0,3},{1,0},{2,1},{3,2},{4,7},{5,4},{6,5},{7,6},{8,11},{9,8},{10,9... | collective-permute-start | bytes 1474568 | tf_op jit(solution)/shard_map/ppermute | solution.py:309
  117.4 34.4 %collective-permute-start.10 = (bf16[256,1280]{1,0:T(8,128)(2,1)}, bf16[256,1280]{1,0:T(8,128)(2,1)S(1)}, u32[]{:S(2)}, u32[]{:S(2)}) collective-permute-start(bf16[256,1280]{1,0:T(8,128)(2,1)} %slice.70), channel_id=1, source_target_pairs={{0,1},{1,2},{2,3},{3,0},{4,5},{5,6},{6,7},{7,4},{8,9},{9,10},{10,1... | collective-permute-start | bytes 1966088 | tf_op jit(solution)/shard_map/ppermute | solution.py:308
  122.1 34.9 %collective-permute-start.11 = (bf16[256,1280]{1,0:T(8,128)(2,1)}, bf16[256,1280]{1,0:T(8,128)(2,1)}, u32[]{:S(2)}, u32[]{:S(2)}) collective-permute-start(bf16[256,1280]{1,0:T(8,128)(2,1)} %slice.71), channel_id=1, source_target_pairs={{0,3},{1,0},{2,1},{3,2},{4,7},{5,4},{6,5},{7,6},{8,11},{9,8},{10,9... | collective-permute-start | bytes 1966088 | tf_op jit(solution)/shard_map/ppermute | solution.py:309
  168.1 13.4 %copy-start.2 = (bf16[512,256]{1,0:T(8,128)(2,1)S(1)}, bf16[512,256]{1,0:T(8,128)(2,1)}, u32[]{:S(2)}) copy-start(bf16[512,256]{1,0:T(8,128)(2,1)} %get-tuple-element.10.refs_1_) | copy-start | bytes 786436
  168.1 13.4 %copy-start.6 = (bf16[384,256]{1,0:T(8,128)(2,1)S(1)}, bf16[384,256]{1,0:T(8,128)(2,1)}, u32[]{:S(2)}) copy-start(bf16[384,256]{1,0:T(8,128)(2,1)} %get-tuple-element.11.refs_2_) | copy-start | bytes 589828
  184.8 144.3 %all-to-all-start.1 = ((bf16[32,2,64,256]{3,2,1,0:T(8,128)(2,1)}), bf16[32,2,64,256]{3,2,1,0:T(8,128)(2,1)}, u32[]{:S(2)}, u32[]{:S(2)}) async-start(bf16[32,2,64,256]{3,2,1,0:T(8,128)(2,1)} %broadcast_select_fusion), calls=%async_computation.1 | async-start | bytes 4194304 | tf_op jit(solution)/shard_map/all_to_all | solution.py:368
  (7 other events, 26.6 us)
